TPU v7x, 32 devices: a whole 2x2x4 slice. The times are simulated.
32 devices in a mesh: seq: 2 (over x), fsdp: 4 (over z), replica: 4 (over y, core).
Axes of the slice: x: 2, y: 2, z: 4, core: 2. Of those that a mesh axis runs over, the one named last changes fastest.
Arguments:
- latent_tokens: bfloat16 [32, 1024, 1152], P(('fsdp', 'replica'), 'seq'), may hold values from -6 to 6
- conditioning: bfloat16 [32, 1152], P(('fsdp', 'replica')), may hold values from -6 to 6
- ada_weight: bfloat16 [1152, 6912], P(('seq', 'fsdp')), may hold values from -0.1875 to 0.1875
- ada_bias: bfloat16 [6912], P(('seq', 'fsdp')), may hold values from -2 to 2
- qkv_weight: bfloat16 [1152, 3456], P(('seq', 'fsdp')), may hold values from -0.1875 to 0.1875
- qv_bias: bfloat16 [2304], P(('seq', 'fsdp')), may hold values from -2 to 2
- out_weight: bfloat16 [1152, 1152], P(('seq', 'fsdp')), may hold values from -3 to 3
- out_bias: bfloat16 [1152], P(('seq', 'fsdp')), may hold values from -2 to 2
- up_weight: bfloat16 [1152, 4608], P(('seq', 'fsdp')), may hold values from -0.1875 to 0.1875
- up_bias: bfloat16 [4608], P(('seq', 'fsdp')), may hold values from -2 to 2
- down_weight: bfloat16 [4608, 1152], P(('seq', 'fsdp')), may hold values from -0.09375 to 0.09375
- down_bias: bfloat16 [1152], P(('seq', 'fsdp')), may hold values from -2 to 2
- out_cotangent: bfloat16 [32, 1024, 1152], P(('fsdp', 'replica'), 'seq'), may hold values from -6 to 6
Outputs:
- block_out: bfloat16 [32, 1024, 1152], P(('fsdp', 'replica'), 'seq')
- tokens_grad: float32 [32, 1024, 1152], P(('fsdp', 'replica'), 'seq')
- cond_grad: float32 [32, 1152], P(('fsdp', 'replica'))
- ada_wgrad: float32 [1152, 6912], P(('seq', 'fsdp'))
- ada_bgrad: float32 [6912], P(('seq', 'fsdp'))
- qkv_wgrad: float32 [1152, 3456], P(('seq', 'fsdp'))
- qv_bgrad: float32 [2304], P(('seq', 'fsdp'))
- out_wgrad: float32 [1152, 1152], P(('seq', 'fsdp'))
- out_bgrad: float32 [1152], P(('seq', 'fsdp'))
- up_wgrad: float32 [1152, 4608], P(('seq', 'fsdp'))
- up_bgrad: float32 [4608], P(('seq', 'fsdp'))
- down_wgrad: float32 [4608, 1152], P(('seq', 'fsdp'))
- down_bgrad: float32 [1152], P(('seq', 'fsdp'))
All inputs are finite; a program needn't handle non-finite values.
Results may differ from a plain program's by a relative error of at most 0.02.
The roundings to bfloat16 on the way count: a program that leaves them out, or rounds other values in their place, can miss the bound.
Values may be sent and summed in bfloat16 or wider, within the bound.
A program may use at most 384 MiB of HBM per device.

v0:
```python
import math

import jax
import jax.numpy as jnp
from jax import lax
from jax.sharding import PartitionSpec as P

HEADS = 16
HEAD_DIM = 72


def norm_mod(values, shift, scale):
    centre = values - jnp.mean(values, axis=-1, keepdims=True)
    spread = jnp.mean(centre * centre, axis=-1, keepdims=True)
    return centre * lax.rsqrt(spread + 1e-06) * (1.0 + scale) + shift


def gelu_tanh(values):
    return jax.nn.gelu(values, approximate=True)


def split_heads(values):
    return values.reshape(values.shape[0], HEADS, HEAD_DIM)


def attend_forward(trio):
    query, keys, values = trio
    scale_factor = 1.0 / math.sqrt(HEAD_DIM)
    scores = (
        jnp.einsum(
            "qhd,khd->hqk",
            split_heads(query),
            split_heads(keys),
            preferred_element_type=jnp.float32,
        )
        * scale_factor
    )
    top = jnp.max(scores, axis=-1, keepdims=True)
    expo = jnp.exp(scores - top)
    total = jnp.sum(expo, axis=-1, keepdims=True)
    probs = (expo / total).astype(jnp.bfloat16)
    attended = jnp.einsum(
        "hqk,khd->qhd", probs, split_heads(values), preferred_element_type=jnp.float32
    )
    log_total = (top + jnp.log(total))[:, :, 0]
    return (attended.reshape(query.shape[0], -1).astype(jnp.bfloat16), log_total)


def attend_backward(group):
    query, keys, values, grad_att, log_total = group
    scale_factor = 1.0 / math.sqrt(HEAD_DIM)
    q_heads = split_heads(query)
    k_heads = split_heads(keys)
    v_heads = split_heads(values)
    g_heads = split_heads(grad_att)
    scores = (
        jnp.einsum("qhd,khd->hqk", q_heads, k_heads, preferred_element_type=jnp.float32)
        * scale_factor
    )
    probs = jnp.exp(scores - log_total[:, :, None])
    d_probs = jnp.einsum("qhd,khd->hqk", g_heads, v_heads, preferred_element_type=jnp.float32)
    delta = jnp.sum(probs * d_probs, axis=-1, keepdims=True)
    d_scores = (probs * (d_probs - delta)).astype(jnp.bfloat16)
    d_query = (
        jnp.einsum("hqk,khd->qhd", d_scores, k_heads, preferred_element_type=jnp.float32)
        * scale_factor
    )
    d_keys = (
        jnp.einsum("hqk,qhd->khd", d_scores, q_heads, preferred_element_type=jnp.float32)
        * scale_factor
    )
    d_values = jnp.einsum(
        "hqk,qhd->khd", probs.astype(jnp.bfloat16), g_heads, preferred_element_type=jnp.float32
    )
    return (
        d_query.reshape(query.shape[0], -1),
        d_keys.reshape(keys.shape[0], -1),
        d_values.reshape(keys.shape[0], -1),
    )


def project(left, right):
    return jnp.einsum("ltd,de->lte", left, right, preferred_element_type=jnp.float32)


def project_back(left, right):
    return jnp.einsum("lte,de->ltd", left, right, preferred_element_type=jnp.float32)


def weight_term(left, right):
    return jnp.einsum("ltd,lte->de", left, right, preferred_element_type=jnp.float32)


def bias_term(grad):
    return jnp.sum(grad.astype(jnp.float32), axis=(0, 1))


def body(
    latent_tokens,
    conditioning,
    ada_weight,
    ada_bias,
    qkv_weight,
    qv_bias,
    out_weight,
    out_bias,
    up_weight,
    up_bias,
    down_weight,
    down_bias,
    out_cotangent,
):
    gathered = (
        lax.all_gather(ada_weight, ("seq", "fsdp"), axis=0, tiled=True),
        lax.all_gather(ada_bias, ("seq", "fsdp"), axis=0, tiled=True),
        lax.all_gather(qkv_weight, ("seq", "fsdp"), axis=0, tiled=True),
        lax.all_gather(qv_bias, ("seq", "fsdp"), axis=0, tiled=True),
        lax.all_gather(out_weight, ("seq", "fsdp"), axis=0, tiled=True),
        lax.all_gather(out_bias, ("seq", "fsdp"), axis=0, tiled=True),
        lax.all_gather(up_weight, ("seq", "fsdp"), axis=0, tiled=True),
        lax.all_gather(up_bias, ("seq", "fsdp"), axis=0, tiled=True),
        lax.all_gather(down_weight, ("seq", "fsdp"), axis=0, tiled=True),
        lax.all_gather(down_bias, ("seq", "fsdp"), axis=0, tiled=True),
    )
    w_ada, b_ada, w_qkv, b_qv, w_out, b_out, w_up, b_up, w_down, b_down = gathered
    width = latent_tokens.shape[2]
    cond32 = conditioning.astype(jnp.float32)
    activated = jax.nn.silu(cond32).astype(jnp.bfloat16)
    modulation = jnp.dot(activated, w_ada, preferred_element_type=jnp.float32) + b_ada.astype(
        jnp.float32
    )
    pieces = [modulation[:, None, index * width : (index + 1) * width] for index in range(6)]
    shift_a, scale_a, gate_a, shift_m, scale_m, gate_m = pieces
    tokens32 = latent_tokens.astype(jnp.float32)
    attn_in = norm_mod(tokens32, shift_a, scale_a).astype(jnp.bfloat16)
    bias_qv = b_qv.astype(jnp.float32)
    bias_full = jnp.concatenate(
        [bias_qv[:width], jnp.zeros((width,), jnp.float32), bias_qv[width:]]
    )
    projected = (project(attn_in, w_qkv) + bias_full).astype(jnp.bfloat16)
    query = projected[:, :, :width]
    keys = projected[:, :, width : 2 * width]
    values = projected[:, :, 2 * width :]
    keys_all, values_all = (
        lax.all_gather(keys, "seq", axis=1, tiled=True),
        lax.all_gather(values, "seq", axis=1, tiled=True),
    )
    attended, log_total = lax.map(attend_forward, (query, keys_all, values_all))
    branch = project(attended, w_out) + b_out.astype(jnp.float32)
    middle = tokens32 + gate_a * branch
    mlp_in = norm_mod(middle, shift_m, scale_m).astype(jnp.bfloat16)
    pre_act = project(mlp_in, w_up) + b_up.astype(jnp.float32)
    hidden = gelu_tanh(pre_act).astype(jnp.bfloat16)
    mlp_out = project(hidden, w_down) + b_down.astype(jnp.float32)
    block_out = (middle + gate_m * mlp_out).astype(jnp.bfloat16)
    back_set = (
        lax.all_gather(ada_weight, ("seq", "fsdp"), axis=0, tiled=True),
        lax.all_gather(ada_bias, ("seq", "fsdp"), axis=0, tiled=True),
        lax.all_gather(qkv_weight, ("seq", "fsdp"), axis=0, tiled=True),
        lax.all_gather(qv_bias, ("seq", "fsdp"), axis=0, tiled=True),
        lax.all_gather(out_weight, ("seq", "fsdp"), axis=0, tiled=True),
        lax.all_gather(out_bias, ("seq", "fsdp"), axis=0, tiled=True),
        lax.all_gather(up_weight, ("seq", "fsdp"), axis=0, tiled=True),
        lax.all_gather(up_bias, ("seq", "fsdp"), axis=0, tiled=True),
        lax.all_gather(down_weight, ("seq", "fsdp"), axis=0, tiled=True),
        lax.all_gather(down_bias, ("seq", "fsdp"), axis=0, tiled=True),
    )
    k_ada, k_bias_ada, k_qkv, k_bias_qv, k_out, k_bias_out, k_up, k_bias_up, k_down, k_bias_down = (
        back_set
    )
    grad_out = out_cotangent.astype(jnp.float32)
    d_gate_m = jnp.sum(grad_out * mlp_out, axis=1, keepdims=True)
    d_mlp_out = (grad_out * gate_m).astype(jnp.bfloat16)
    down_term = weight_term(hidden, d_mlp_out)
    down_bias_term = bias_term(d_mlp_out)
    d_hidden = project_back(d_mlp_out, k_down)
    unused_value, gelu_pull = jax.vjp(gelu_tanh, pre_act)
    d_pre = gelu_pull(d_hidden)[0].astype(jnp.bfloat16)
    up_term = weight_term(mlp_in, d_pre)
    up_bias_term = bias_term(d_pre)
    d_mlp_in = project_back(d_pre, k_up)
    unused_norm, norm_pull_m = jax.vjp(norm_mod, middle, shift_m, scale_m)
    d_middle_part, d_shift_m, d_scale_m = norm_pull_m(d_mlp_in)
    d_middle = grad_out + d_middle_part
    d_gate_a = jnp.sum(d_middle * branch, axis=1, keepdims=True)
    d_branch = (d_middle * gate_a).astype(jnp.bfloat16)
    out_term = weight_term(attended, d_branch)
    out_bias_term = bias_term(d_branch)
    d_attended = project_back(d_branch, k_out).astype(jnp.bfloat16)
    d_query, d_keys_all, d_values_all = lax.map(
        attend_backward, (query, keys_all, values_all, d_attended, log_total)
    )
    d_keys, d_values = (
        lax.psum_scatter(
            d_keys_all.astype(jnp.bfloat16), "seq", scatter_dimension=1, tiled=True
        ).astype(jnp.float32),
        lax.psum_scatter(
            d_values_all.astype(jnp.bfloat16), "seq", scatter_dimension=1, tiled=True
        ).astype(jnp.float32),
    )
    d_projected = jnp.concatenate([d_query, d_keys, d_values], axis=-1).astype(jnp.bfloat16)
    qkv_term = weight_term(attn_in, d_projected)
    projected_sums = bias_term(d_projected)
    qv_bias_term = jnp.concatenate([projected_sums[:width], projected_sums[2 * width :]])
    d_attn_in = project_back(d_projected, k_qkv)
    unused_first, norm_pull_a = jax.vjp(norm_mod, tokens32, shift_a, scale_a)
    d_tokens_part, d_shift_a, d_scale_a = norm_pull_a(d_attn_in)
    tokens_grad = d_middle + d_tokens_part
    d_mod_part = jnp.concatenate(
        [d_shift_a, d_scale_a, d_gate_a, d_shift_m, d_scale_m, d_gate_m], axis=-1
    )[:, 0, :]
    d_modulation = lax.psum(d_mod_part.astype(jnp.bfloat16), "seq")
    first_only = (lax.axis_index("seq") == 0).astype(jnp.float32)
    ada_term = jnp.dot(activated.T, d_modulation, preferred_element_type=jnp.float32) * first_only
    ada_bias_term = jnp.sum(d_modulation.astype(jnp.float32), axis=0) * first_only
    sigmoid_cond = jax.nn.sigmoid(cond32)
    silu_slope = sigmoid_cond * (1.0 + cond32 * (1.0 - sigmoid_cond))
    cond_grad = (
        jnp.einsum("le,de->ld", d_modulation, k_ada, preferred_element_type=jnp.float32)
        * silu_slope
    )
    owned = (
        lax.psum_scatter(
            ada_term.astype(jnp.bfloat16), ("seq", "fsdp"), scatter_dimension=0, tiled=True
        ).astype(jnp.float32),
        lax.psum_scatter(
            ada_bias_term.astype(jnp.bfloat16), ("seq", "fsdp"), scatter_dimension=0, tiled=True
        ).astype(jnp.float32),
        lax.psum_scatter(
            qkv_term.astype(jnp.bfloat16), ("seq", "fsdp"), scatter_dimension=0, tiled=True
        ).astype(jnp.float32),
        lax.psum_scatter(
            qv_bias_term.astype(jnp.bfloat16), ("seq", "fsdp"), scatter_dimension=0, tiled=True
        ).astype(jnp.float32),
        lax.psum_scatter(
            out_term.astype(jnp.bfloat16), ("seq", "fsdp"), scatter_dimension=0, tiled=True
        ).astype(jnp.float32),
        lax.psum_scatter(
            out_bias_term.astype(jnp.bfloat16), ("seq", "fsdp"), scatter_dimension=0, tiled=True
        ).astype(jnp.float32),
        lax.psum_scatter(
            up_term.astype(jnp.bfloat16), ("seq", "fsdp"), scatter_dimension=0, tiled=True
        ).astype(jnp.float32),
        lax.psum_scatter(
            up_bias_term.astype(jnp.bfloat16), ("seq", "fsdp"), scatter_dimension=0, tiled=True
        ).astype(jnp.float32),
        lax.psum_scatter(
            down_term.astype(jnp.bfloat16), ("seq", "fsdp"), scatter_dimension=0, tiled=True
        ).astype(jnp.float32),
        lax.psum_scatter(
            down_bias_term.astype(jnp.bfloat16), ("seq", "fsdp"), scatter_dimension=0, tiled=True
        ).astype(jnp.float32),
    )
    summed = (
        lax.psum(owned[0].astype(jnp.bfloat16), "replica").astype(jnp.float32),
        lax.psum(owned[1].astype(jnp.bfloat16), "replica").astype(jnp.float32),
        lax.psum(owned[2].astype(jnp.bfloat16), "replica").astype(jnp.float32),
        lax.psum(owned[3].astype(jnp.bfloat16), "replica").astype(jnp.float32),
        lax.psum(owned[4].astype(jnp.bfloat16), "replica").astype(jnp.float32),
        lax.psum(owned[5].astype(jnp.bfloat16), "replica").astype(jnp.float32),
        lax.psum(owned[6].astype(jnp.bfloat16), "replica").astype(jnp.float32),
        lax.psum(owned[7].astype(jnp.bfloat16), "replica").astype(jnp.float32),
        lax.psum(owned[8].astype(jnp.bfloat16), "replica").astype(jnp.float32),
        lax.psum(owned[9].astype(jnp.bfloat16), "replica").astype(jnp.float32),
    )
    return (
        block_out,
        tokens_grad,
        cond_grad,
        summed[0],
        summed[1],
        summed[2],
        summed[3],
        summed[4],
        summed[5],
        summed[6],
        summed[7],
        summed[8],
        summed[9],
    )


def solution(mesh):
    in_specs = (
        P(("fsdp", "replica"), "seq", None),
        P(("fsdp", "replica"), None),
        P(("seq", "fsdp"), None),
        P(("seq", "fsdp")),
        P(("seq", "fsdp"), None),
        P(("seq", "fsdp")),
        P(("seq", "fsdp"), None),
        P(("seq", "fsdp")),
        P(("seq", "fsdp"), None),
        P(("seq", "fsdp")),
        P(("seq", "fsdp"), None),
        P(("seq", "fsdp")),
        P(("fsdp", "replica"), "seq", None),
    )
    out_specs = (
        P(("fsdp", "replica"), "seq", None),
        P(("fsdp", "replica"), "seq", None),
        P(("fsdp", "replica"), None),
        P(("seq", "fsdp"), None),
        P(("seq", "fsdp")),
        P(("seq", "fsdp"), None),
        P(("seq", "fsdp")),
        P(("seq", "fsdp"), None),
        P(("seq", "fsdp")),
        P(("seq", "fsdp"), None),
        P(("seq", "fsdp")),
        P(("seq", "fsdp"), None),
        P(("seq", "fsdp")),
    )
    return jax.shard_map(body, mesh=mesh, in_specs=in_specs, out_specs=out_specs, check_vma=False)
```

profile of v0, /device:TPU:0, one launch (start us, length us, event | category | flops | bytes accessed | tf_op | source)
XLA Modules:
  0.0 2287.7 jit_solution(14074089410219000438)
XLA Ops:
  17.0 42.5 %all-reduce.11 = (bf16[2304]{0:T(1024)(128)(2,1)S(1)}, bf16[6912]{0:T(1024)(128)(2,1)S(1)}, bf16[1152]{0:T(1024)(128)(2,1)S(1)}, bf16[1152]{0:T(1024)(128)(2,1)}, bf16[4608]{0:T(1024)(128)(2,1)S(1)}) all-reduce(bf16[2304]{0:T(1024)(128)(2,1)S(1)} %dynamic-update-slice.1, ...), channel_id=1, replica_groups=mesh['seq'=2,'fsdp'=4,'replica'=4] {'seq','fsdp'}, use_global_device_ids=true, to_apply=%add.1 | all-reduce | flops 16128 | bytes 64512
  61.3 170.7 %all-gather.8.cloned.1.call-done = bf16[1152,6912]{1,0:T(8,128)(2,1)} async-done(((bf16[144,6912]{1,0:T(8,128)(2,1)}), bf16[1152,6912]{1,0:T(8,128)(2,1)}) %all-gather.8.cloned.1.call-update) | async-done | bytes 15925264 | tf_op jit(solution)/shard_map/all_gather | solution.py:114
  240.4 111.6 %all-gather.10.cloned.1.call-done = bf16[1152,3456]{1,0:T(8,128)(2,1)} async-done(((bf16[144,3456]{1,0:T(8,128)(2,1)}), bf16[1152,3456]{1,0:T(8,128)(2,1)}) %all-gather.10.cloned.1.call-update) | async-done | bytes 7962640 | tf_op jit(solution)/shard_map/all_gather | solution.py:116
  374.4 54.3 %all-gather.14.cloned.1.call-done = bf16[2,1024,1152]{2,1,0:T(8,128)(2,1)} async-done(((bf16[2,512,1152]{2,1,0:T(8,128)(2,1)}), bf16[2,1024,1152]{2,1,0:T(8,128)(2,1)}) %all-gather.14.cloned.1.call-update) | async-done | bytes 4718608 | tf_op jit(solution)/shard_map/all_gather | solution.py:145
  435.3 58.0 %all-gather.12.cloned.1.call-done = bf16[2,1024,1152]{2,1,0:T(8,128)(2,1)} async-done(((bf16[2,512,1152]{2,1,0:T(8,128)(2,1)}), bf16[2,1024,1152]{2,1,0:T(8,128)(2,1)}) %all-gather.12.cloned.1.call-update) | async-done | bytes 4718608 | tf_op jit(solution)/shard_map/all_gather | solution.py:146
  500.0 95.9 %while.26 = (s32[]{:T(128)}, bf16[2,512,1152]{1,2,0:T(8,128)(2,1)}, f32[2,16,512]{2,1,0:T(8,128)S(1)}, bf16[2,1024,1152]{1,2,0:T(8,128)(2,1)}, bf16[2,512,1152]{...) while((s32[]{:T(128)}, bf16[2,512,1152]{1,2,0:T(8,128)(2,1)}, f32[2,16,512]{2,1,0:T(8,128)S(1)}, ...), condition=%wide.region_5.6_spmd, body=%wide.region_2.5_spmd.sunk | while | flops 2491998208 | bytes 141033648 | solution.py:148
  607.2 96.3 %all-gather.18.cloned.1.call-done = bf16[1152,4608]{1,0:T(8,128)(2,1)} async-done(((bf16[144,4608]{1,0:T(8,128)(2,1)}), bf16[1152,4608]{1,0:T(8,128)(2,1)}) %all-gather.18.cloned.1.call-update) | async-done | bytes 10616848 | tf_op jit(solution)/shard_map/all_gather | solution.py:120
  703.5 32.9 %fusion.25 = f32[2,512,4608]{2,1,0:T(8,128)} fusion(bf16[1152,4608]{1,0:T(8,128)(2,1)} %all-gather.18.cloned.1.call-done, f32[2,512,1152]{2,1,0:T(8,128)} %copy-done.6, f32[2,1152]{1,0:T(2,128)S(1)} %copy-done.46, f32[2,1152]{1,0:T(2,128)S(1)} %copy-done.26, f32[2,512]{1,0:T(2,128)S(1)} %fusion.62, f32[2,512]{1,0:T(2,128)S(1)} %broadcast_multiply_fusion.1), kind=kOutput, calls=%fused_computation.53 | convolution fusion | flops 10877534208 | bytes 34236416 | tf_op jit(solution)/shard_map/ltd,de->lte/dot_general | solution.py:83
  736.4 119.9 %all-gather.20.cloned.1.call-done = bf16[4608,1152]{1,0:T(8,128)(2,1)} async-done(((bf16[576,1152]{1,0:T(8,128)(2,1)}), bf16[4608,1152]{1,0:T(8,128)(2,1)}) %all-gather.20.cloned.1.call-update) | async-done | bytes 10616848 | tf_op jit(solution)/shard_map/all_gather | solution.py:122
  856.3 28.9 %fusion.76 = (bf16[4608]{0:T(1024)(128)(2,1)}, bf16[2,512,4608]{2,1,0:T(8,128)(2,1)}) fusion(f32[2,512,4608]{2,1,0:T(8,128)} %fusion.25, f32[4608]{0:T(1024)S(1)} %copy-done.33, bf16[4608,1152]{1,0:T(8,128)(2,1)} %all-gather.20.cloned.1.call-done, bf16[2,512,1152]{2,1,0:T(8,128)(2,1)S(1)} %copy-done.8, f32[2,1152]{1,0:T(2,128)S(1)} %copy-done.22), kind=kOutput, calls=%fused_computation.139 | convolution fusion | flops 10978979840 | bytes 41324544 | tf_op jit(solution)/shard_map/lte,de->ltd/dot_general | solution.py:87
  919.4 253.8 %while.27 = (s32[]{:T(128)}, bf16[2,512,1152]{2,1,0:T(8,128)(2,1)}, bf16[2,1024,1152]{2,1,0:T(8,128)(2,1)}, bf16[2,1024,1152]{2,1,0:T(8,128)(2,1)}, bf16[2,1024,...) while((s32[]{:T(128)}, bf16[2,512,1152]{2,1,0:T(8,128)(2,1)}, ...), condition=%wide.region_12.13_spmd, body=%wide.region_10.12_spmd.sunk | while | flops 6143991808 | bytes 343245056 | solution.py:190
  961.7 25.2 %multiply_reduce_fusion.9 = (f32[16,512]{1,0:T(8,128)}, f32[16,512,1024]{2,1,0:T(8,128)}) fusion(f32[16,512,1024]{2,1,0:T(8,128)} %fusion.132, f32[16,512]{1,0:T(8,128)} %dynamic-slice_bitcast_fusion.2, bf16[512,16,72]{0,2,1:T(8,128)(2,1)} %bitcast.168, bf16[1024,16,72]{0,2,1:T(8,128)(2,1)} %bitcast.166), kind=kOutput, calls=%fused_computation.13.clone.1 | convolution fusion | flops 1241505792 | bytes 70713344 | tf_op jit(solution)/shard_map/while/body/eval_jaxpr/qhd,khd->hqk/dot_general | solution.py:61
  986.9 28.0 %multiply_convert_fusion.9 = bf16[16,512,1024]{2,1,0:T(8,128)(2,1)} fusion(f32[16,512,1024]{2,1,0:T(8,128)} %get-tuple-element.345, f32[16,512,1024]{2,1,0:T(8,128)} %fusion.132, f32[16,512]{1,0:T(8,128)} %get-tuple-element.346, f32[16,512]{1,0:T(8,128)} %dynamic-slice_bitcast_fusion.2), kind=kLoop, calls=%fused_computation.12.clone.1 | loop fusion | flops 41943040 | bytes 83951616 | tf_op jit(solution)/shard_map/while/body/eval_jaxpr/convert_element_type | solution.py:63
  1088.4 25.2 %multiply_reduce_fusion.9 = (f32[16,512]{1,0:T(8,128)}, f32[16,512,1024]{2,1,0:T(8,128)}) fusion(f32[16,512,1024]{2,1,0:T(8,128)} %fusion.132, f32[16,512]{1,0:T(8,128)} %dynamic-slice_bitcast_fusion.2, bf16[512,16,72]{0,2,1:T(8,128)(2,1)} %bitcast.168, bf16[1024,16,72]{0,2,1:T(8,128)(2,1)} %bitcast.166), kind=kOutput, calls=%fused_computation.13.clone.1 | convolution fusion | flops 1241505792 | bytes 70713344 | tf_op jit(solution)/shard_map/while/body/eval_jaxpr/qhd,khd->hqk/dot_general | solution.py:61
  1113.6 28.0 %multiply_convert_fusion.9 = bf16[16,512,1024]{2,1,0:T(8,128)(2,1)} fusion(f32[16,512,1024]{2,1,0:T(8,128)} %get-tuple-element.345, f32[16,512,1024]{2,1,0:T(8,128)} %fusion.132, f32[16,512]{1,0:T(8,128)} %get-tuple-element.346, f32[16,512]{1,0:T(8,128)} %dynamic-slice_bitcast_fusion.2), kind=kLoop, calls=%fused_computation.12.clone.1 | loop fusion | flops 41943040 | bytes 83951616 | tf_op jit(solution)/shard_map/while/body/eval_jaxpr/convert_element_type | solution.py:63
  1201.4 23.1 %fusion.11 = bf16[4608,1152]{1,0:T(8,128)(2,1)} fusion(bf16[2,512,1152]{2,1,0:T(8,128)(2,1)S(1)} %copy-done.9, f32[2,1152]{1,0:T(2,128)S(1)} %copy-done.23, f32[2,512,4608]{2,1,0:T(8,128)} %fusion.25, f32[4608]{0:T(1024)S(1)} %copy-done.34), kind=kOutput, calls=%fused_computation.36 | convolution fusion | flops 10927669248 | bytes 31878144 | tf_op jit(solution)/shard_map/ltd,lte->de/dot_general | solution.py:91
  1231.6 62.4 %reduce-scatter.8.cloned.1.call-done = bf16[2,512,1152]{2,1,0:T(8,128)(2,1)} async-done(((bf16[2,1024,1152]{2,1,0:T(8,128)(2,1)}), bf16[2,512,1152]{2,1,0:T(8,128)(2,1)}) %reduce-scatter.8.cloned.1.call-update) | async-done | bytes 2359312 | tf_op jit(solution)/shard_map/reduce_scatter | solution.py:194
  1329.6 26.7 %fusion.46 = (bf16[2,1152]{1,0:T(2,128)(2,1)S(1)}, bf16[2,1152]{1,0:T(2,128)(2,1)S(1)}, f32[2,512,1152]{2,1,0:T(8,128)}, bf16[2,512,1152]{2,1,0:T(8,128)(2,1)}) fusion(bf16[2,512,1152]{2,1,0:T(8,128)(2,1)} %param.29, f32[2,512,1152]{2,1,0:T(8,128)} %get-tuple-element.235, f32[2,512,1152]{2,1,0:T(8,128)} %copy-done.7, f32[2,512]{1,0:T(2,128)S(1)} %copy-done.40, ...), kind=kOutput, calls=%fused_computation.83 | convolution fusion | flops 10942410752 | bytes 60233216 | tf_op jit(solution)/shard_map/ltd,de->lte/dot_general | solution.py:83
  1371.5 180.2 %reduce-scatter.18.cloned.1.call-done = bf16[144,4608]{1,0:T(8,128)(2,1)} async-done(((bf16[1152,4608]{1,0:T(8,128)(2,1)}), bf16[144,4608]{1,0:T(8,128)(2,1)}) %reduce-scatter.18.cloned.1.call-update) | async-done | bytes 1327120 | tf_op jit(solution)/shard_map/reduce_scatter | solution.py:241
  1551.7 182.5 %reduce-scatter.20.cloned.1.call-done = bf16[576,1152]{1,0:T(8,128)(2,1)} async-done(((bf16[4608,1152]{1,0:T(8,128)(2,1)}), bf16[576,1152]{1,0:T(8,128)(2,1)}) %reduce-scatter.20.cloned.1.call-update) | async-done | bytes 1327120 | tf_op jit(solution)/shard_map/reduce_scatter | solution.py:247
  1734.2 145.8 %reduce-scatter.14.cloned.1.call-done = bf16[144,3456]{1,0:T(8,128)(2,1)} async-done(((bf16[1152,3456]{1,0:T(8,128)(2,1)}), bf16[144,3456]{1,0:T(8,128)(2,1)}) %reduce-scatter.14.cloned.1.call-update) | async-done | bytes 995344 | tf_op jit(solution)/shard_map/reduce_scatter | solution.py:229
  1880.1 272.6 %reduce-scatter.12.cloned.1.call-done = bf16[144,6912]{1,0:T(8,128)(2,1)} async-done(((bf16[1152,6912]{1,0:T(8,128)(2,1)}), bf16[144,6912]{1,0:T(8,128)(2,1)}) %reduce-scatter.12.cloned.1.call-update) | async-done | bytes 1990672 | tf_op jit(solution)/shard_map/reduce_scatter | solution.py:223
  2159.2 35.9 %all-reduce.10 = (bf16[6912]{0:T(1024)(128)(2,1)S(1)}, bf16[2304]{0:T(1024)(128)(2,1)S(1)}, bf16[1152]{0:T(1024)(128)(2,1)S(1)}, bf16[4608]{0:T(1024)(128)(2,1)S(1)}, bf16[1152]{0:T(1024)(128)(2,1)S(1)}) all-reduce(bf16[6912]{0:T(1024)(128)(2,1)S(1)} %multiply_convert_fusion.4,, ...), channel_id=5, replica_groups=mesh['seq'=2,'fsdp'=4,'replica'=4] {'seq','fsdp'}, use_global_device_ids=true, to_apply=%region_27.28.clone | all-reduce | flops 16128 | bytes 64512
  2215.7 54.6 %all-reduce.16.cloned.1.call-done = (bf16[144,6912]{1,0:T(8,128)(2,1)}, bf16[144,3456]{1,0:T(8,128)(2,1)}, bf16[144,1152]{1,0:T(8,128)(2,1)}, bf16[144,4608]{1,0:T(8,128)(2,1)}, bf16[576,1152]{1,0:T(8,128)(2,1)}) async-done(((bf16[144,6912]{1,0:T(8,128)(2,1)}, bf16[144,3456]{1,0:T(8,128)(2,1)}, bf16[144,1152]{1,0:T(8,128)(2,1)}, bf16[144,4608]{1,0:T(8,128)(2,1)}, bf16[576,1152]{1,0:T(8,128)(2,1)}), ...) | async-done | bytes 5971984 | tf_op jit(solution)/shard_map/psum | solution.py:255
  (282 shorter events, 461.4 us)
Async XLA Ops:
  7.2 224.9 %copy-start.18 = (bf16[2,1152]{1,0:T(2,128)(2,1)S(1)}, bf16[2,1152]{1,0:T(2,128)(2,1)}, u32[]{:S(2)}) copy-start(bf16[2,1152]{1,0:T(2,128)(2,1)} %param.18) | copy-start | bytes 13828
  7.2 224.9 %all-gather.8.cloned.1.call-start = ((), (), s32[]{:S(2)}) async-start(), calls=%async_computation.7 | async-start | bytes 17915904 | tf_op jit(solution)/shard_map/all_gather | solution.py:114
  7.9 344.1 %all-gather.10.cloned.1.call-start = ((), (), s32[]{:S(2)}) async-start(), calls=%async_computation.8 | async-start | bytes 8957952 | tf_op jit(solution)/shard_map/all_gather | solution.py:116
  8.7 420.0 %all-gather.14.cloned.1.call-start = ((), (), s32[]{:S(2)}) async-start(), calls=%async_computation.10 | async-start | bytes 7077888 | tf_op jit(solution)/shard_map/all_gather | solution.py:145
  59.9 292.1 %copy-start.20 = (f32[2,512]{1,0:T(2,128)}, f32[2,512]{1,0:T(2,128)S(1)}, u32[]{:S(2)}) copy-start(f32[2,512]{1,0:T(2,128)S(1)} %broadcast_multiply_fusion.2) | copy-start | bytes 12292
  61.3 290.7 %copy-start.37 = (f32[2,512]{1,0:T(2,128)}, f32[2,512]{1,0:T(2,128)S(1)}, u32[]{:S(2)}) copy-start(f32[2,512]{1,0:T(2,128)S(1)} %fusion.61) | copy-start | bytes 12292
  367.7 125.7 %all-gather.12.cloned.1.call-start = ((), (), s32[]{:S(2)}) async-start(), calls=%async_computation.9 | async-start | bytes 7077888 | tf_op jit(solution)/shard_map/all_gather | solution.py:146
  368.3 227.6 %all-gather.16.cloned.1.call-start = ((), (), s32[]{:S(2)}) async-start(), calls=%async_computation.11 | async-start | bytes 2985984 | tf_op jit(solution)/shard_map/all_gather | solution.py:118
  368.9 334.6 %all-gather.18.cloned.1.call-start = ((), (), s32[]{:S(2)}) async-start(), calls=%async_computation.12 | async-start | bytes 11943936 | tf_op jit(solution)/shard_map/all_gather | solution.py:120
  369.5 486.8 %all-gather.20.cloned.1.call-start = ((), (), s32[]{:S(2)}) async-start(), calls=%async_computation.13 | async-start | bytes 11943936 | tf_op jit(solution)/shard_map/all_gather | solution.py:122
  370.2 861.4 %reduce-scatter.10.cloned.1.call-start = ((), (), s32[]{:S(2)}) async-start(), calls=%async_computation.15 | async-start | bytes 7077888 | tf_op jit(solution)/shard_map/reduce_scatter | solution.py:197
  604.5 301.9 %copy-start.31 = (f32[2,512]{1,0:T(2,128)}, f32[2,512]{1,0:T(2,128)S(1)}, u32[]{:S(2)}) copy-start(f32[2,512]{1,0:T(2,128)S(1)} %broadcast_multiply_fusion.1) | copy-start | bytes 12292
  607.2 299.2 %copy-start.41 = (f32[2,512]{1,0:T(2,128)}, f32[2,512]{1,0:T(2,128)S(1)}, u32[]{:S(2)}) copy-start(f32[2,512]{1,0:T(2,128)S(1)} %fusion.62) | copy-start | bytes 12292
  703.5 152.8 %copy-start.8 = (bf16[2,512,1152]{2,1,0:T(8,128)(2,1)S(1)}, bf16[2,512,1152]{2,1,0:T(8,128)(2,1)}, u32[]{:S(2)}) copy-start(bf16[2,512,1152]{2,1,0:T(8,128)(2,1)} %param.29) | copy-start | bytes 7077892
  703.5 152.8 %copy-start.22 = (f32[2,1152]{1,0:T(2,128)S(1)}, f32[2,1152]{1,0:T(2,128)}, u32[]{:S(2)}) copy-start(f32[2,1152]{1,0:T(2,128)} %get-tuple-element.223) | copy-start | bytes 27652
  703.5 152.8 %copy-start.33 = (f32[4608]{0:T(1024)S(1)}, f32[4608]{0:T(1024)}, u32[]{:S(2)}) copy-start(f32[4608]{0:T(1024)} %convert_element_type.185) | copy-start | bytes 55300
  1173.2 120.8 %reduce-scatter.8.cloned.1.call-start = ((), (), s32[]{:S(2)}) async-start(), calls=%async_computation.14 | async-start | bytes 7077888 | tf_op jit(solution)/shard_map/reduce_scatter | solution.py:194
  1174.0 197.5 %reduce-scatter.16.cloned.1.call-start = ((), (), s32[]{:S(2)}) async-start(), calls=%async_computation.18 | async-start | bytes 2985984 | tf_op jit(solution)/shard_map/reduce_scatter | solution.py:235
  1181.3 370.4 %reduce-scatter.18.cloned.1.call-start = ((), (), s32[]{:S(2)}) async-start(), calls=%async_computation.19 | async-start | bytes 11943936 | tf_op jit(solution)/shard_map/reduce_scatter | solution.py:241
  1199.6 534.6 %reduce-scatter.20.cloned.1.call-start = ((), (), s32[]{:S(2)}) async-start(), calls=%async_computation.20 | async-start | bytes 11943936 | tf_op jit(solution)/shard_map/reduce_scatter | solution.py:247
  1224.5 655.5 %reduce-scatter.14.cloned.1.call-start = ((), (), s32[]{:S(2)}) async-start(), calls=%async_computation.17 | async-start | bytes 8957952 | tf_op jit(solution)/shard_map/reduce_scatter | solution.py:229
  1308.6 844.0 %reduce-scatter.12.cloned.1.call-start = ((), (), s32[]{:S(2)}) async-start(), calls=%async_computation.16 | async-start | bytes 17915904 | tf_op jit(solution)/shard_map/reduce_scatter | solution.py:223
  1371.4 783.9 %copy-start.10 = (bf16[2,512,1152]{2,1,0:T(8,128)(2,1)S(1)}, bf16[2,512,1152]{2,1,0:T(8,128)(2,1)}, u32[]{:S(2)}) copy-start(bf16[2,512,1152]{2,1,0:T(8,128)(2,1)} %reduce-scatter.10.cloned.1.call-done) | copy-start | bytes 7077892
  1371.4 898.8 %all-reduce.16.cloned.1.call-start = ((), (), s32[]{:S(2)}) async-start(), calls=%async_computation.21 | async-start | bytes 11943936 | tf_op jit(solution)/shard_map/psum | solution.py:255
  (53 other events, 1399.2 us)
Sparse Core Ops, SparseCore 0:
  10.1 221.8 all-gather.7
  234.2 117.7 all-gather.9
  367.8 60.8 all-gather.13
  430.7 62.6 all-gather.11
  495.3 55.0 all-gather.15
  552.4 151.0 all-gather.17
  705.6 150.6 all-gather.19
  1173.4 58.1 reduce-scatter.9
  1234.0 59.9 reduce-scatter.7
  1298.1 70.5 reduce-scatter.15
  1372.7 178.9 reduce-scatter.17
  1555.2 179.0 reduce-scatter.19
  1738.3 141.7 reduce-scatter.13
  1884.3 268.2 reduce-scatter.11
  2155.5 114.7 all-reduce.15
where the time goes:
time: 2300 us; the launch traced here: 2290 us
  waiting for transfers between devices  1520 us (66%)
  matrix products  445 us (19%)
  other arithmetic  116 us (5%)
  blocking collectives  92.4 us (4%)
  local copies, waits for them, and re-layouts  91.8 us (4%)
    reduce_scatter x1, waiting for transfers between devices, body(): lax.psum_scatter(ada_term.astype(jnp.bfloat16), ('seq', 'fsdp'), scatter_...  273 us
    reduce_scatter x1, waiting for transfers between devices, body(): lax.psum_scatter(down_term.astype(jnp.bfloat16), ('seq', 'fsdp'), scatter...  183 us
    reduce_scatter x1, waiting for transfers between devices, body(): lax.psum_scatter(up_term.astype(jnp.bfloat16), ('seq', 'fsdp'), scatter_d...  180 us
    all_gather x1, waiting for transfers between devices, body(): lax.all_gather(ada_weight, ('seq', 'fsdp'), axis=0, tiled=True)  171 us
    reduce_scatter x1, waiting for transfers between devices, body(): lax.psum_scatter(qkv_term.astype(jnp.bfloat16), ('seq', 'fsdp'), scatter_...  146 us
    all_gather x1, waiting for transfers between devices, body(): lax.all_gather(down_weight, ('seq', 'fsdp'), axis=0, tiled=True)  120 us
    all_gather x1, waiting for transfers between devices, body(): lax.all_gather(qkv_weight, ('seq', 'fsdp'), axis=0, tiled=True)  112 us
    all_gather x1, waiting for transfers between devices, body(): lax.all_gather(up_weight, ('seq', 'fsdp'), axis=0, tiled=True)  96.3 us
  transfers between devices with their start and end apart: 15, of which 13 were waited for; matrix products, arithmetic and copies ran while one was open for 13% of the time, Pallas kernels for 0%

commit v1 on v0

v1 whole, which is shorter than its diff:
```python
import functools
import math

import jax
import jax.numpy as jnp
from jax import lax
from jax.experimental import pallas as pl
from jax.experimental.pallas import tpu as pltpu
from jax.sharding import PartitionSpec as P

HEADS = 16
HEAD_DIM = 72
PAIR = 2
PAIRS = HEADS // PAIR
ROWS = PAIR * HEAD_DIM
OWNERS = ("seq", "fsdp")
EVERY = ("seq", "fsdp", "replica")
SCALE = 1.0 / math.sqrt(HEAD_DIM)
SCALE2 = SCALE * math.log2(math.e)


def norm_mod(values, shift, scale):
    centre = values - jnp.mean(values, axis=-1, keepdims=True)
    spread = jnp.mean(centre * centre, axis=-1, keepdims=True)
    return centre * lax.rsqrt(spread + 1e-06) * (1.0 + scale) + shift


def gelu_tanh(values):
    return jax.nn.gelu(values, approximate=True)


def mm(left, right, dims):
    return lax.dot_general(left, right, (dims, ((), ())), preferred_element_type=jnp.float32)


def forward_kernel(parts, *refs):
    q_ref, k_refs, v_refs = refs[0], refs[1 : 1 + parts], refs[1 + parts : 1 + 2 * parts]
    out_ref, log_ref = refs[1 + 2 * parts :]
    outs, logs = [], []
    for head in range(PAIR):
        rows = slice(head * HEAD_DIM, (head + 1) * HEAD_DIM)
        query = q_ref[0][rows]
        scores = [mm(k[0][rows], query, ((0,), (0,))) * SCALE2 for k in k_refs]
        top = functools.reduce(jnp.maximum, [jnp.max(s, axis=0, keepdims=True) for s in scores])
        expo = [jnp.exp2(s - top) for s in scores]
        total = functools.reduce(jnp.add, [jnp.sum(e, axis=0, keepdims=True) for e in expo])
        inverse = 1.0 / total
        outs.append(
            sum(
                mm(v[0][rows], (e * inverse).astype(jnp.bfloat16), ((1,), (0,)))
                for v, e in zip(v_refs, expo)
            )
        )
        logs.append(top + jnp.log2(total))
    out_ref[0] = jnp.concatenate(outs, axis=0).astype(out_ref.dtype)
    log_ref[0, 0] = jnp.concatenate(logs, axis=0)


def backward_kernel(parts, *refs):
    q_ref, k_refs, v_refs = refs[0], refs[1 : 1 + parts], refs[1 + parts : 1 + 2 * parts]
    g_ref, log_ref = refs[1 + 2 * parts : 3 + 2 * parts]
    dq_ref, dk_refs, dv_refs = (
        refs[3 + 2 * parts],
        refs[4 + 2 * parts : 4 + 3 * parts],
        refs[4 + 3 * parts :],
    )
    dqs, dks, dvs = [], [[] for _ in range(parts)], [[] for _ in range(parts)]
    for head in range(PAIR):
        rows = slice(head * HEAD_DIM, (head + 1) * HEAD_DIM)
        query, grad = q_ref[0][rows], g_ref[0][rows]
        log_total = log_ref[0, 0, head : head + 1, :]
        probs, weighted = [], []
        for part in range(parts):
            scores = mm(k_refs[part][0][rows], query, ((0,), (0,))) * SCALE2
            prob = jnp.exp2(scores - log_total)
            d_prob = mm(v_refs[part][0][rows], grad, ((0,), (0,)))
            probs.append(prob)
            weighted.append(d_prob)
            dvs[part].append(mm(grad, prob.astype(jnp.bfloat16), ((1,), (1,))))
        delta = sum(jnp.sum(p * d, axis=0, keepdims=True) for p, d in zip(probs, weighted))
        d_query = 0.0
        for part in range(parts):
            d_score = (probs[part] * (weighted[part] - delta)).astype(jnp.bfloat16)
            d_query = d_query + mm(k_refs[part][0][rows], d_score, ((1,), (0,)))
            dks[part].append(mm(query, d_score, ((1,), (1,))) * SCALE)
        dqs.append(d_query * SCALE)
    dq_ref[0] = jnp.concatenate(dqs, axis=0).astype(dq_ref.dtype)
    for part in range(parts):
        dk_refs[part][0] = jnp.concatenate(dks[part], axis=0).astype(dq_ref.dtype)
        dv_refs[part][0] = jnp.concatenate(dvs[part], axis=0).astype(dq_ref.dtype)


def block(tokens, offset):
    return pl.BlockSpec((1, ROWS, tokens), lambda latent, pair: (latent, pair + offset, 0))


def attend_forward(projected, others):
    latents, width3, tokens = projected.shape
    width = width3 // 3
    parts = 1 + len(others)
    k_specs = [block(tokens, PAIRS)] + [block(tokens, 0)] * len(others)
    v_specs = [block(tokens, 2 * PAIRS)] + [block(tokens, PAIRS)] * len(others)
    log_spec = pl.BlockSpec((1, 1, PAIR, tokens), lambda latent, pair: (latent, pair, 0, 0))
    work = latents * HEADS * tokens * tokens * parts
    return pl.pallas_call(
        functools.partial(forward_kernel, parts),
        grid=(latents, PAIRS),
        in_specs=[block(tokens, 0)] + k_specs + v_specs,
        out_specs=[block(tokens, 0), log_spec],
        out_shape=[
            jax.ShapeDtypeStruct((latents, width, tokens), jnp.bfloat16),
            jax.ShapeDtypeStruct((latents, PAIRS, PAIR, tokens), jnp.float32),
        ],
        compiler_params=pltpu.CompilerParams(vmem_limit_bytes=40 * 1024 * 1024),
        cost_estimate=pl.CostEstimate(
            flops=12 * 128 * work, bytes_accessed=8 * projected.size, transcendentals=work
        ),
    )(projected, projected, *others, projected, *others)


def attend_backward(projected, others, grad, log_total):
    latents, width3, tokens = projected.shape
    width = width3 // 3
    parts = 1 + len(others)
    k_specs = [block(tokens, PAIRS)] + [block(tokens, 0)] * len(others)
    v_specs = [block(tokens, 2 * PAIRS)] + [block(tokens, PAIRS)] * len(others)
    log_spec = pl.BlockSpec((1, 1, PAIR, tokens), lambda latent, pair: (latent, pair, 0, 0))
    work = latents * HEADS * tokens * tokens * parts
    outs = pl.pallas_call(
        functools.partial(backward_kernel, parts),
        grid=(latents, PAIRS),
        in_specs=[block(tokens, 0)] + k_specs + v_specs + [block(tokens, 0), log_spec],
        out_specs=[block(tokens, 0)] * (1 + 2 * parts),
        out_shape=[jax.ShapeDtypeStruct((latents, width, tokens), jnp.bfloat16)] * (1 + 2 * parts),
        compiler_params=pltpu.CompilerParams(vmem_limit_bytes=48 * 1024 * 1024),
        cost_estimate=pl.CostEstimate(
            flops=30 * 128 * work, bytes_accessed=16 * projected.size, transcendentals=work
        ),
    )(projected, projected, *others, projected, *others, grad, log_total)
    return outs[0], outs[1 : 1 + parts], outs[1 + parts :]


def gather_blocks(weight, width):
    rows, cols = weight.shape
    if cols != width * lax.axis_size("replica"):
        return lax.all_gather(weight, OWNERS, axis=0, tiled=True)
    mine = lax.dynamic_slice_in_dim(weight, lax.axis_index("replica") * width, width, 1)
    blocks = lax.all_gather(mine, EVERY, axis=0, tiled=True)
    blocks = blocks.reshape(-1, cols // width, rows, width)
    return jnp.swapaxes(blocks, 1, 2).reshape(-1, cols)


def gather_rows(weight, width):
    rows, count = weight.shape[0], lax.axis_size("replica")
    if rows % (16 * count):
        return lax.all_gather(weight, OWNERS, axis=0, tiled=True)
    share = rows // count
    mine = lax.dynamic_slice_in_dim(weight, lax.axis_index("replica") * share, share, 0)
    return lax.all_gather(mine, EVERY, axis=0, tiled=True)


def sum_plain(term):
    owned = lax.psum_scatter(term, OWNERS, scatter_dimension=0, tiled=True)
    return lax.psum(owned, "replica")


def sum_blocks(term, width):
    cols, count, owners = term.shape[1], lax.axis_size("replica"), lax.axis_size(OWNERS)
    if cols != width * count:
        return sum_plain(term)
    blocks = jnp.swapaxes(term.reshape(owners, -1, count, width), 1, 2).reshape(-1, width)
    owned = lax.psum_scatter(blocks, EVERY, scatter_dimension=0, tiled=True)
    owned = lax.all_gather(owned, "replica", axis=0, tiled=False)
    return jnp.swapaxes(owned, 0, 1).reshape(-1, cols)


def sum_rows(term):
    if term.shape[0] % (16 * lax.axis_size(EVERY)):
        return sum_plain(term)
    owned = lax.psum_scatter(term, EVERY, scatter_dimension=0, tiled=True)
    return lax.all_gather(owned, "replica", axis=0, tiled=True)


def shift_seq(values, step):
    count = lax.axis_size("seq")
    return lax.ppermute(values, "seq", [(i, (i + step) % count) for i in range(count)])


def bias_term(grad, axes):
    return jnp.sum(grad.astype(jnp.float32), axis=axes)


def body(
    latent_tokens,
    conditioning,
    ada_weight,
    ada_bias,
    qkv_weight,
    qv_bias,
    out_weight,
    out_bias,
    up_weight,
    up_bias,
    down_weight,
    down_bias,
    out_cotangent,
):
    width = latent_tokens.shape[2]
    latents = latent_tokens.shape[0]
    seq_size, fsdp_size = lax.axis_size("seq"), lax.axis_size("fsdp")
    replica_size = lax.axis_size("replica")
    owner = lax.axis_index("seq") * fsdp_size + lax.axis_index("fsdp")
    owners = seq_size * fsdp_size
    fsdp_at, replica_at = lax.axis_index("fsdp"), lax.axis_index("replica")
    wide = ada_weight.shape[1]
    ada_rows = ada_weight.shape[0]

    cond32 = conditioning.astype(jnp.float32)
    activated = jax.nn.silu(cond32).astype(jnp.bfloat16)
    act_all = lax.all_gather(activated, ("fsdp", "replica"), axis=0, tiled=True)
    act_rows = lax.dynamic_slice_in_dim(act_all, owner * ada_rows, ada_rows, 1)

    def of_group(values):
        split = values.reshape((fsdp_size, replica_size, latents) + values.shape[1:])
        return lax.dynamic_index_in_dim(split, replica_at, 1, keepdims=False)

    act_group = of_group(act_rows).reshape(fsdp_size * latents, ada_rows)
    partial_mod = jnp.dot(act_group, ada_weight, preferred_element_type=jnp.float32)

    def placed(bias):
        zeros = jnp.zeros((owners * bias.shape[0],), jnp.float32)
        return lax.dynamic_update_slice_in_dim(
            zeros, bias.astype(jnp.float32), owner * bias.shape[0], 0
        )

    partial_mod = partial_mod + placed(ada_bias)[None, :]
    biases = jnp.concatenate([placed(b) for b in (qv_bias, out_bias, up_bias, down_bias)])
    bias_rows = -(-biases.shape[0] // wide)
    biases = jnp.pad(biases, (0, bias_rows * wide - biases.shape[0])).reshape(bias_rows, wide)
    small = lax.psum(jnp.concatenate([partial_mod, biases], axis=0), OWNERS)
    modulation = lax.dynamic_slice_in_dim(small, fsdp_at * latents, latents, 0)
    flat = small[fsdp_size * latents :].reshape(-1)
    hidden_units = up_weight.shape[1]
    b_qv = flat[: 2 * width]
    b_out = flat[2 * width : 3 * width]
    b_up = flat[3 * width : 3 * width + hidden_units]
    b_down = flat[3 * width + hidden_units : 4 * width + hidden_units]

    w_attn = gather_blocks(jnp.concatenate([qkv_weight, out_weight], axis=1), width)
    w_qkv, w_out = w_attn[:, : 3 * width], w_attn[:, 3 * width :]
    w_up = gather_blocks(up_weight, width)
    w_down = gather_rows(down_weight, width)

    pieces = [modulation[:, None, index * width : (index + 1) * width] for index in range(6)]
    shift_a, scale_a, gate_a, shift_m, scale_m, gate_m = pieces
    tokens32 = latent_tokens.astype(jnp.float32)
    attn_in = norm_mod(tokens32, shift_a, scale_a).astype(jnp.bfloat16)
    bias_full = jnp.concatenate([b_qv[:width], jnp.zeros((width,), jnp.float32), b_qv[width:]])

    def ein(form, left, right):
        return jnp.einsum(form, left, right, preferred_element_type=jnp.float32)

    projected = (ein("ltd,de->let", attn_in, w_qkv) + bias_full[None, :, None]).astype(jnp.bfloat16)
    own_kv = projected[:, width:, :]
    others = [shift_seq(own_kv, step) for step in range(1, seq_size)]
    attended, log_total = attend_forward(projected, others)
    branch = ein("ldt,de->lte", attended, w_out) + b_out
    middle = tokens32 + gate_a * branch
    mlp_in = norm_mod(middle, shift_m, scale_m).astype(jnp.bfloat16)
    pre_act = ein("ltd,de->lte", mlp_in, w_up) + b_up
    hidden = gelu_tanh(pre_act).astype(jnp.bfloat16)
    mlp_out = ein("ltd,de->lte", hidden, w_down) + b_down
    block_out = (middle + gate_m * mlp_out).astype(jnp.bfloat16)

    grad_out = out_cotangent.astype(jnp.float32)
    d_gate_m = jnp.sum(grad_out * mlp_out, axis=1, keepdims=True)
    d_mlp_out = (grad_out * gate_m).astype(jnp.bfloat16)
    down_term = ein("ltd,lte->de", hidden, d_mlp_out).astype(jnp.bfloat16)
    down_bias_term = bias_term(d_mlp_out, (0, 1))
    down_term, d_mlp_out = lax.optimization_barrier((down_term, d_mlp_out))
    down_grad = sum_rows(down_term)
    d_hidden = ein("lte,de->ltd", d_mlp_out, w_down)
    unused_value, gelu_pull = jax.vjp(gelu_tanh, pre_act)
    d_pre = gelu_pull(d_hidden)[0].astype(jnp.bfloat16)
    up_term = ein("ltd,lte->de", mlp_in, d_pre).astype(jnp.bfloat16)
    up_bias_term = bias_term(d_pre, (0, 1))
    up_term, d_pre = lax.optimization_barrier((up_term, d_pre))
    up_grad = sum_blocks(up_term, width)
    d_mlp_in = ein("lte,de->ltd", d_pre, w_up)
    unused_norm, norm_pull_m = jax.vjp(norm_mod, middle, shift_m, scale_m)
    d_middle_part, d_shift_m, d_scale_m = norm_pull_m(d_mlp_in)
    d_middle = grad_out + d_middle_part
    d_gate_a = jnp.sum(d_middle * branch, axis=1, keepdims=True)
    d_branch = (d_middle * gate_a).astype(jnp.bfloat16)
    out_term = ein("ldt,lte->de", attended, d_branch).astype(jnp.bfloat16)
    out_bias_term = bias_term(d_branch, (0, 1))
    out_term, d_branch = lax.optimization_barrier((out_term, d_branch))
    d_attended = ein("lte,de->ldt", d_branch, w_out).astype(jnp.bfloat16)
    d_query, d_key_parts, d_value_parts = attend_backward(projected, others, d_attended, log_total)
    d_kv = jnp.concatenate([d_key_parts[0], d_value_parts[0]], axis=1).astype(jnp.float32)
    for step in range(1, seq_size):
        there = jnp.concatenate([d_key_parts[step], d_value_parts[step]], axis=1)
        d_kv = d_kv + shift_seq(there, -step).astype(jnp.float32)
    d_projected = jnp.concatenate([d_query, d_kv.astype(jnp.bfloat16)], axis=1)
    qkv_term = ein("ltd,let->de", attn_in, d_projected).astype(jnp.bfloat16)
    projected_sums = bias_term(d_projected, (0, 2))
    qv_bias_term = jnp.concatenate([projected_sums[:width], projected_sums[2 * width :]])
    qkv_term, d_projected = lax.optimization_barrier((qkv_term, d_projected))
    attn_grad = sum_blocks(jnp.concatenate([qkv_term, out_term], axis=1), width)
    qkv_grad, out_grad = attn_grad[:, : 3 * width], attn_grad[:, 3 * width :]
    d_attn_in = ein("let,de->ltd", d_projected, w_qkv)
    unused_first, norm_pull_a = jax.vjp(norm_mod, tokens32, shift_a, scale_a)
    d_tokens_part, d_shift_a, d_scale_a = norm_pull_a(d_attn_in)
    tokens_grad = d_middle + d_tokens_part
    d_mod_part = jnp.concatenate(
        [d_shift_a, d_scale_a, d_gate_a, d_shift_m, d_scale_m, d_gate_m], axis=-1
    )[:, 0, :]
    bias_terms = jnp.concatenate([qv_bias_term, out_bias_term, up_bias_term, down_bias_term])
    bias_terms = jnp.pad(bias_terms, (0, bias_rows * wide - bias_terms.shape[0]))
    mine = jnp.concatenate([d_mod_part, bias_terms.reshape(bias_rows, wide)], axis=0)
    every = lax.all_gather(mine.astype(jnp.bfloat16), EVERY, axis=0, tiled=False)
    every = every.astype(jnp.float32)
    d_modulation = jnp.sum(
        every[:, :latents].reshape((seq_size, -1, wide)), axis=0
    ).astype(jnp.bfloat16)
    bias_sums = jnp.sum(every[:, latents:], axis=0).reshape(-1)
    ada_wgrad = jnp.einsum("ld,le->de", act_rows, d_modulation, preferred_element_type=jnp.float32)

    def owned(values, start, count):
        return lax.dynamic_slice_in_dim(values, start + owner * (count // owners), count // owners, 0)

    ada_bgrad = owned(jnp.sum(d_modulation.astype(jnp.float32), axis=0), 0, wide)
    qv_bgrad = owned(bias_sums, 0, 2 * width)
    out_bgrad = owned(bias_sums, 2 * width, width)
    up_bgrad = owned(bias_sums, 3 * width, hidden_units)
    down_bgrad = owned(bias_sums, 3 * width + hidden_units, width)

    d_group = of_group(d_modulation).reshape(fsdp_size * latents, wide)
    cond_part = jnp.einsum("le,de->ld", d_group, ada_weight, preferred_element_type=jnp.float32)
    cond_parts = lax.all_gather(cond_part, OWNERS, axis=0, tiled=False)
    cond_mine = lax.dynamic_slice_in_dim(cond_parts, fsdp_at * latents, latents, 1)
    cond_mine = jnp.swapaxes(cond_mine, 0, 1).reshape(latents, -1)
    sigmoid_cond = jax.nn.sigmoid(cond32)
    silu_slope = sigmoid_cond * (1.0 + cond32 * (1.0 - sigmoid_cond))
    cond_grad = cond_mine * silu_slope
    return (
        block_out,
        tokens_grad,
        cond_grad,
        ada_wgrad,
        ada_bgrad,
        qkv_grad.astype(jnp.float32),
        qv_bgrad,
        out_grad.astype(jnp.float32),
        out_bgrad,
        up_grad.astype(jnp.float32),
        up_bgrad,
        down_grad.astype(jnp.float32),
        down_bgrad,
    )


def solution(mesh):
    in_specs = (
        P(("fsdp", "replica"), "seq", None),
        P(("fsdp", "replica"), None),
        P(("seq", "fsdp"), None),
        P(("seq", "fsdp")),
        P(("seq", "fsdp"), None),
        P(("seq", "fsdp")),
        P(("seq", "fsdp"), None),
        P(("seq", "fsdp")),
        P(("seq", "fsdp"), None),
        P(("seq", "fsdp")),
        P(("seq", "fsdp"), None),
        P(("seq", "fsdp")),
        P(("fsdp", "replica"), "seq", None),
    )
    out_specs = (
        P(("fsdp", "replica"), "seq", None),
        P(("fsdp", "replica"), "seq", None),
        P(("fsdp", "replica"), None),
        P(("seq", "fsdp"), None),
        P(("seq", "fsdp")),
        P(("seq", "fsdp"), None),
        P(("seq", "fsdp")),
        P(("seq", "fsdp"), None),
        P(("seq", "fsdp")),
        P(("seq", "fsdp"), None),
        P(("seq", "fsdp")),
        P(("seq", "fsdp"), None),
        P(("seq", "fsdp")),
    )
    return jax.shard_map(body, mesh=mesh, in_specs=in_specs, out_specs=out_specs, check_vma=False)
```

time: 2300 us -> 1050 us (0.46)
  waiting for transfers between devices: 1520 us -> 470 us
  matrix products: 445 us -> 215 us
  Pallas kernels: 0 us -> 89.3 us
  other arithmetic: 116 us -> 68.1 us
  local copies, waits for them, and re-layouts: 91.8 us -> 132 us
  blocking collectives: 92.4 us -> 53.9 us
    reduce_scatter x7 -> x3, waiting for transfers between devices: 851 us -> 108 us  [the longest x2 108 us: sum_blocks(): owned = lax.psum_scatter(blocks, EVERY, scatter_dimension=0, tiled=True)]
    all_gather x7, waiting for transfers between devices: 611 us -> 134 us  [the longest x2 70.9 us: gather_blocks(): blocks = lax.all_gather(mine, EVERY, axis=0, tiled=True)]
    dot_general x29 -> x15, matrix products: 445 us -> 215 us  [the longest x12 211 us: ein(): return jnp.einsum(form, left, right, preferred_element_type=jnp.float32)]
    ppermute x0 -> x2, waiting for transfers between devices: none -> 144 us  [shift_seq(): lax.ppermute(values, 'seq', [(i, (i + step) % count) for i in range(count)])]
    reshape x0 -> x16, local copies, waits for them, and re-layouts: none -> 98.2 us  [the longest x4 50.5 us: sum_blocks(): term.reshape(owners, -1, count, width)]
    pallas_call x0 -> x2, Pallas kernels: none -> 89.3 us  [the longest x1 55.1 us: attend_backward(): pl.pallas_call(functools.partial(backward_kernel, parts), grid=(latents,...]
    unnamed x2 -> x0, blocking collectives: 78.4 us -> none
    convert_element_type x17 -> x5, other arithmetic: 70.8 us -> 14.4 us  [the longest x1 7.42 us: body(): d_projected = jnp.concatenate([d_query, d_kv.astype(jnp.bfloat16)], axis=1)]
  transfers between devices with their start and end apart: 15 -> 13, of which waited for: 13 -> 9; matrix products, arithmetic and copies ran while one was open for 13% -> 31% of each run, Pallas kernels for 0% -> 9%
where the time goes in v1:
time: 1050 us
  waiting for transfers between devices  470 us (45%)
  matrix products  215 us (20%)
  local copies, waits for them, and re-layouts  132 us (13%)
  Pallas kernels  89.3 us (9%)
  other arithmetic  68.1 us (6%)
  blocking collectives  53.9 us (5%)
  between operations  16.6 us (2%)
    dot_general x12, matrix products, ein(): return jnp.einsum(form, left, right, preferred_element_type=jnp.float32)  211 us
    ppermute x2, waiting for transfers between devices, shift_seq(): lax.ppermute(values, 'seq', [(i, (i + step) % count) for i in range(count)])  144 us
    reduce_scatter x2, waiting for transfers between devices, sum_blocks(): owned = lax.psum_scatter(blocks, EVERY, scatter_dimension=0, tiled=True)  108 us
    psum x1, waiting for transfers between devices, body(): small = lax.psum(jnp.concatenate([partial_mod, biases], axis=0), OWNERS)  83 us
    all_gather x2, waiting for transfers between devices, gather_blocks(): blocks = lax.all_gather(mine, EVERY, axis=0, tiled=True)  70.9 us
    pallas_call x1, Pallas kernels, attend_backward(): pl.pallas_call(functools.partial(backward_kernel, parts), grid=(latents,...  55.1 us
    reshape x4, local copies, waits for them, and re-layouts, sum_blocks(): term.reshape(owners, -1, count, width)  50.5 us
    pallas_call x1, Pallas kernels, attend_forward(): pl.pallas_call(functools.partial(forward_kernel, parts), grid=(latents, P...  34.2 us
  transfers between devices with their start and end apart: 13, of which 9 were waited for; matrix products, arithmetic and copies ran while one was open for 31% of the time, Pallas kernels for 9%

profile of v1, /device:TPU:0, one launch (start us, length us, event | category | flops | bytes accessed | tf_op | source)
XLA Modules:
  0.0 1046.4 jit_solution(271042000266799437)
XLA Ops:
  12.1 23.3 %all-gather.3 = bf16[16,2,1152]{2,1,0:T(2,128)(2,1)S(1)} all-gather(bf16[1,2,1152]{2,1,0:T(2,128)(2,1)S(1)} %fusion.45), channel_id=1, replica_groups=mesh['seq'=2,'fsdp'=4,'replica'=4] {'fsdp','replica'}, dimensions={0}, use_global_device_ids=true | all-gather | bytes 78336 | tf_op jit(solution)/shard_map/all_gather | solution.py:220
  47.4 83.0 %all-reduce.4.cloned.1.call-done = f32[10,6912]{1,0:T(8,128)} async-done(((f32[10,6912]{1,0:T(8,128)}), f32[10,6912]{1,0:T(8,128)}) %all-reduce.4.cloned.1.call-update) | async-done | bytes 276496 | tf_op jit(solution)/shard_map/psum | solution.py:240
  168.9 70.9 %all-gather.14.cloned.1.call-done = bf16[4608,1152]{1,0:T(8,128)(2,1)} async-done(((bf16[144,1152]{1,0:T(8,128)(2,1)}), bf16[4608,1152]{1,0:T(8,128)(2,1)}) %all-gather.14.cloned.1.call-update) | async-done | bytes 10616848 | tf_op jit(solution)/shard_map/all_gather | solution.py:148
  239.8 18.4 %copy.105 = bf16[8,4,144,1152]{3,1,2,0:T(4,128)(2,1)} copy(bf16[8,4,144,1152]{3,2,1,0:T(8,128)(2,1)} %bitcast.116) | data formatting | bytes 21233664 | tf_op jit(solution)/shard_map/reshape | solution.py:149
  258.2 15.4 %reshape.230 = bf16[1152,4608,1]{1,0,2:T(8,128)(2,1)} reshape(bf16[8,144,4,1152]{3,2,1,0:T(4,128)(2,1)} %bitcast.111) | data formatting | bytes 21233664 | tf_op jit(solution)/shard_map/reshape | solution.py:150
  273.6 27.5 %collective-permute-done.refs_2_.refs_4_ = bf16[2,2304,512]{2,1,0:T(8,128)(2,1)} collective-permute-done((bf16[2,2304,512]{2,1,0:T(8,128)(2,1)}, bf16[2,2304,512]{2,1,0:T(8,128)(2,1)}, u32[]{:S(2)}, u32[]{:S(2)}) %collective-permute-start) | collective-permute-done | bytes 4718624 | tf_op jit(solution)/shard_map/ppermute | solution.py:186
  304.2 34.2 %shard_map.228 = (bf16[2,1152,512]{2,1,0:T(8,128)(2,1)S(1)}, f32[2,8,2,512]{3,2,1,0:T(2,128)S(1)}) custom-call(bf16[2,3456,512]{2,1,0:T(8,128)(2,1)S(1)} %copy-done.2, bf16[2,3456,512]{2,1,0:T(8,128)(2,1)S(1)} %copy-done.2, bf16[2,2304,512]{2,1,0:T(8,128)(2,1)} %collective-permute-done.refs_2_.refs_4_, bf16[2,3456,512]{2,1,0:T(8,128)(2,1)S(1)} %copy-done.2, ...), custom_call_target="tpu_custom_call" | custom-call | flops 25769803776 | bytes 28311552 | tf_op jit(solution)/shard_map/pallas_call | solution.py:105
  338.4 18.3 %fusion.53 = (f32[2,512]{1,0:T(2,128)S(1)}, f32[2,512,1152]{2,1,0:T(8,128)S(1)}, f32[2,512,1152]{2,1,0:T(8,128)}) fusion(f32[2,1152]{1,0:T(2,128)S(1)} %get-tuple-element.67, bf16[2,512,1152]{2,1,0:T(8,128)(2,1)S(1)} %copy-done.9, f32[1152]{0:T(1024)S(1)} %get-tuple-element.72, bf16[2,1152,512]{2,1,0:T(8,128)(2,1)S(1)} %get-tuple-element.28, ...), kind=kOutput, calls=%fused_computation.128 | convolution fusion | flops 2723806208 | bytes 16827904 | tf_op jit(solution)/shard_map/ldt,de->lte/dot_general | solution.py:261
  357.4 20.4 %fusion.37 = f32[2,512,4608]{2,1,0:T(8,128)} fusion(bf16[1152,4608,1]{1,0,2:T(8,128)(2,1)} %reshape.230, f32[2,512,1152]{2,1,0:T(8,128)S(1)} %get-tuple-element.58, f32[2,1152]{1,0:T(2,128)S(1)} %get-tuple-element.68, f32[2,1152]{1,0:T(2,128)S(1)} %get-tuple-element.64, f32[2,512]{1,0:T(2,128)S(1)} %fusion.47, f32[2,512]{1,0:T(2,128)S(1)} %broadcast_multiply_fusion), kind=kOutput, calls=%fused_computation.80 | convolution fusion | flops 10877534208 | bytes 34236416 | tf_op jit(solution)/shard_map/ltd,de->lte/dot_general | solution.py:261
  377.8 22.9 %fusion.1 = bf16[4608,1152]{1,0:T(8,128)(2,1)} fusion(bf16[2,512,1152]{2,1,0:T(8,128)(2,1)} %get-tuple-element.29, f32[2,512,4608]{2,1,0:T(8,128)} %fusion.37, f32[4608]{0:T(1024)S(1)} %slice.96), kind=kOutput, calls=%fused_computation.5 | convolution fusion | flops 10924130304 | bytes 31868928 | tf_op jit(solution)/shard_map/ltd,lte->de/dot_general | solution.py:261
  400.7 28.8 %fusion.58 = (bf16[4608]{0:T(1024)(128)(2,1)}, bf16[2,512,4608]{2,1,0:T(8,128)(2,1)S(1)}) fusion(f32[2,512,4608]{2,1,0:T(8,128)} %fusion.37, f32[4608]{0:T(1024)S(1)} %slice.96, bf16[2,512,1152]{2,1,0:T(8,128)(2,1)} %get-tuple-element.29, bf16[4608,1152]{1,0:T(8,128)(2,1)} %all-gather.16.cloned.1.call-done), kind=kOutput, calls=%fused_computation.133 | convolution fusion | flops 10975440896 | bytes 41315328 | tf_op jit(solution)/shard_map/lte,de->ltd/dot_general | solution.py:261
  433.0 16.7 %fusion = bf16[1152,4608]{1,0:T(8,128)(2,1)} fusion(bf16[2,512,4608]{2,1,0:T(8,128)(2,1)S(1)} %get-tuple-element.30, f32[2,512,1152]{2,1,0:T(8,128)} %copy-done.12, f32[2,1152]{1,0:T(2,128)S(1)} %get-tuple-element.68, f32[2,1152]{1,0:T(2,128)S(1)} %get-tuple-element.64, f32[2,512]{1,0:T(2,128)S(1)} %fusion.47, f32[2,512]{1,0:T(2,128)S(1)} %broadcast_multiply_fusion), kind=kOutput, calls=%fused_computation.4 | convolution fusion | flops 10882842624 | bytes 24799232 | tf_op jit(solution)/shard_map/ltd,lte->de/dot_general | solution.py:261
  449.8 14.6 %reshape.219 = bf16[8,144,4,1152]{3,2,1,0:T(4,128)(2,1)} reshape(bf16[1152,4608]{1,0:T(8,128)(2,1)} %fusion) | data formatting | bytes 21233664 | tf_op jit(solution)/shard_map/reshape | solution.py:171
  475.1 21.5 %multiply_reduce_fusion = (bf16[2,1152]{1,0:T(2,128)(2,1)}, f32[2,512]{1,0:T(2,128)S(1)}, bf16[2,1152]{1,0:T(2,128)(2,1)}, f32[2,512,1152]{2,1,0:T(8,128)}) fusion(f32[2,512,1152]{2,1,0:T(8,128)} %copy-done.12, f32[2,512]{1,0:T(2,128)S(1)} %fusion.47, f32[2,512]{1,0:T(2,128)S(1)} %broadcast_multiply_fusion, f32[2,1152]{1,0:T(2,128)S(1)} %get-tuple-element.64, ...), kind=kOutput, calls=%fused_computation.53 | convolution fusion | flops 10881068032 | bytes 29521920 | tf_op jit(solution)/shard_map/lte,de->ltd/dot_general | solution.py:261
  516.2 55.1 %shard_map.229 = (bf16[2,1152,512]{2,1,0:T(8,128)(2,1)S(1)}, bf16[2,1152,512]{2,1,0:T(8,128)(2,1)S(1)}, bf16[2,1152,512]{2,1,0:T(8,128)(2,1)}, bf16[2,1152,512]{2,1,0:T(8,128)(2,1)}, bf16[2,1152,512]{2,1,0:T(8,128)(2,1)}) custom-call(bf16[2,3456,512]{2,1,0:T(8,128)(2,1)} %copy-done.1, bf16[2,3456,512]{2,1,0:T(8,128)(2,1)} %copy-done.1, ...), custom_call_target="tpu_custom_call" | custom-call | flops 64424509440 | bytes 56623104 | tf_op jit(solution)/shard_map/pallas_call | solution.py:129
  578.2 116.3 %collective-permute-done.1 = bf16[2,2304,512]{2,1,0:T(8,128)(2,1)} collective-permute-done((bf16[2,2304,512]{2,1,0:T(8,128)(2,1)}, bf16[2,2304,512]{2,1,0:T(8,128)(2,1)}, u32[]{:S(2)}, u32[]{:S(2)}) %collective-permute-start.1) | collective-permute-done | bytes 4718624 | tf_op jit(solution)/shard_map/ppermute | solution.py:186
  709.6 15.8 %fusion.9 = bf16[1152,3456]{1,0:T(8,128)(2,1)} fusion(bf16[2,512,1152]{2,1,0:T(8,128)(2,1)} %param.13, f32[2,1152]{1,0:T(2,128)S(1)} %copy-done.39, f32[2,1152]{1,0:T(2,128)S(1)} %copy-done.26, f32[2,512]{1,0:T(2,128)S(1)} %copy-done.36, f32[2,512]{1,0:T(2,128)S(1)} %copy-done.22, bf16[2,2304,512]{2,1,0:T(8,128)(2,1)} %add_convert_fusion.1, ...), kind=kOutput, calls=%fused_computation.15 | convolution fusion | flops 8178941952 | bytes 17426432 | tf_op jit(solution)/shard_map/ltd,let->de/dot_general | solution.py:261
  725.5 15.8 %fusion.29 = (f32[2,512]{1,0:T(2,128)S(1)}, f32[2,512,1152]{2,1,0:T(8,128)}) fusion(bf16[2,512,1152]{2,1,0:T(8,128)(2,1)S(1)} %copy-done.10, f32[2,1152]{1,0:T(2,128)S(1)} %copy-done.26, f32[2,512]{1,0:T(2,128)S(1)} %copy-done.22, bf16[2,3456,512]{2,1,0:T(8,128)(2,1)S(1)} %copy-done.15, bf16[1152,4608]{1,0:T(8,128)(2,1)} %bitcast.115), kind=kOutput, calls=%fused_computation.49 | convolution fusion | flops 8159624192 | bytes 22135808 | tf_op jit(solution)/shard_map/let,de->ltd/dot_general | solution.py:261
  745.4 26.6 %fusion.31 = (bf16[2,1152]{1,0:T(2,128)(2,1)S(1)}, bf16[2,1152]{1,0:T(2,128)(2,1)S(1)}, f32[2,512,1152]{2,1,0:T(8,128)}, bf16[2,512,1152]{2,1,0:T(8,128)(2,1)}) fusion(bf16[2,512,1152]{2,1,0:T(8,128)(2,1)} %param.25, f32[2,512,1152]{2,1,0:T(8,128)} %get-tuple-element.77, f32[2,512,1152]{2,1,0:T(8,128)} %copy-done.11, ...), kind=kOutput, calls=%fused_computation.51 | convolution fusion | flops 10942410752 | bytes 60233216 | tf_op jit(solution)/shard_map/ltd,de->lte/dot_general | solution.py:261
  809.4 19.6 %all-gather.18.cloned.1.call-done = bf16[32,4,6912]{2,1,0:T(4,128)(2,1)} async-done(((bf16[1,4,6912]{2,1,0:T(4,128)(2,1)}), bf16[32,4,6912]{2,1,0:T(4,128)(2,1)}) %all-gather.18.cloned.1.call-update) | async-done | bytes 1769488 | tf_op jit(solution)/shard_map/all_gather | solution.py:321
  838.8 30.6 %all-gather = f32[64,144]{1,0:T(8,128)S(1)} all-gather(f32[8,144]{1,0:T(8,128)S(1)} %fusion.59), channel_id=2, replica_groups=mesh['seq'=2,'fsdp'=4,'replica'=4] {'seq','fsdp'}, dimensions={0}, use_global_device_ids=true | all-gather | bytes 41472 | tf_op jit(solution)/shard_map/all_gather | solution.py:340
  869.4 107.5 %reduce-scatter.4.cloned.1.call-done = bf16[144,1152]{1,0:T(8,128)(2,1)} async-done(((bf16[4608,1152]{1,0:T(8,128)(2,1)}), bf16[144,1152]{1,0:T(8,128)(2,1)}) %reduce-scatter.4.cloned.1.call-update) | async-done | bytes 331792 | tf_op jit(solution)/shard_map/reduce_scatter | solution.py:172
  998.9 16.4 %all-gather.20.cloned.1.call-done = bf16[576,1152]{1,0:T(8,128)(2,1)} async-done(((bf16[144,1152]{1,0:T(8,128)(2,1)}), bf16[576,1152]{1,0:T(8,128)(2,1)}) %all-gather.20.cloned.1.call-update) | async-done | bytes 1327120 | tf_op jit(solution)/shard_map/all_gather | solution.py:181
  1018.3 16.8 %all-gather.22.cloned.1.call-done = bf16[576,1152]{1,0:T(8,128)(2,1)} async-done(((bf16[144,1152]{1,0:T(8,128)(2,1)}), bf16[576,1152]{1,0:T(8,128)(2,1)}) %all-gather.22.cloned.1.call-update) | async-done | bytes 1327120 | tf_op jit(solution)/shard_map/all_gather | solution.py:173
  (217 shorter events, 193.2 us)
Async XLA Ops:
  8.0 28.4 %copy-start = (bf16[144,6912]{1,0:T(8,128)(2,1)S(1)}, bf16[144,6912]{1,0:T(8,128)(2,1)}, u32[]{:S(2)}) copy-start(bf16[144,6912]{1,0:T(8,128)(2,1)} %param.15) | copy-start | bytes 5971972
  8.0 29.7 %copy-start.16 = (bf16[144,3456]{1,0:T(8,128)(2,1)S(1)}, bf16[144,3456]{1,0:T(8,128)(2,1)}, u32[]{:S(2)}) copy-start(bf16[144,3456]{1,0:T(8,128)(2,1)} %param.17) | copy-start | bytes 2985988
  8.0 122.4 %all-reduce.4.cloned.1.call-start = ((), (), s32[]{:S(2)}) async-start(), calls=%async_computation.3 | async-start | bytes 884736 | tf_op jit(solution)/shard_map/psum | solution.py:240
  37.6 95.5 %all-gather.12.cloned.1.call-start = ((), (), s32[]{:S(2)}) async-start(), calls=%async_computation.4 | async-start | bytes 10948608 | tf_op jit(solution)/shard_map/all_gather | solution.py:148
  38.6 201.2 %all-gather.14.cloned.1.call-start = ((), (), s32[]{:S(2)}) async-start(), calls=%async_computation.5 | async-start | bytes 10948608 | tf_op jit(solution)/shard_map/all_gather | solution.py:148
  40.4 360.3 %all-gather.16.cloned.1.call-start = ((), (), s32[]{:S(2)}) async-start(), calls=%async_computation.6 | async-start | bytes 10948608 | tf_op jit(solution)/shard_map/all_gather | solution.py:159
  42.2 766.1 %reduce-scatter.6.cloned.1.call-start = ((), (), s32[]{:S(2)}) async-start(), calls=%async_computation.9 | async-start | bytes 10948608 | tf_op jit(solution)/shard_map/reduce_scatter | solution.py:172
  44.3 102.4 %copy-start.21 = (f32[2,512]{1,0:T(2,128)}, f32[2,512]{1,0:T(2,128)S(1)}, u32[]{:S(2)}) copy-start(f32[2,512]{1,0:T(2,128)S(1)} %broadcast_multiply_fusion.1) | copy-start | bytes 12292
  47.4 99.4 %copy-start.35 = (f32[2,512]{1,0:T(2,128)}, f32[2,512]{1,0:T(2,128)S(1)}, u32[]{:S(2)}) copy-start(f32[2,512]{1,0:T(2,128)S(1)} %fusion.46) | copy-start | bytes 12292
  133.1 33.2 %copy-start.23 = (f32[2,1152]{1,0:T(2,128)}, f32[2,1152]{1,0:T(2,128)S(1)}, u32[]{:S(2)}) copy-start(f32[2,1152]{1,0:T(2,128)S(1)} %get-tuple-element.63) | copy-start | bytes 27652
  133.1 205.3 %copy-start.19 = (f32[2,1152]{1,0:T(2,128)}, f32[2,1152]{1,0:T(2,128)S(1)}, u32[]{:S(2)}) copy-start(f32[2,1152]{1,0:T(2,128)S(1)} %get-tuple-element.67) | copy-start | bytes 27652
  165.2 136.0 %collective-permute-start = (bf16[2,2304,512]{2,1,0:T(8,128)(2,1)}, bf16[2,2304,512]{2,1,0:T(8,128)(2,1)}, u32[]{:S(2)}, u32[]{:S(2)}) collective-permute-start(bf16[2,2304,512]{2,1,0:T(8,128)(2,1)} %slice.93), channel_id=1, source_target_pairs={{0,16},{16,0},{1,17},{17,1},{2,18},{18,2},{3,19},{19,3},{4,20},{20... | collective-permute-start | bytes 14155784 | tf_op jit(solution)/shard_map/ppermute | solution.py:186
  166.3 234.4 %copy-start.31 = (f32[4608]{0:T(1024)}, f32[4608]{0:T(1024)S(1)}, u32[]{:S(2)}) copy-start(f32[4608]{0:T(1024)S(1)} %slice.96) | copy-start | bytes 55300
  304.2 34.2 %copy-start.9 = (bf16[2,512,1152]{2,1,0:T(8,128)(2,1)S(1)}, bf16[2,512,1152]{2,1,0:T(8,128)(2,1)}, u32[]{:S(2)}) copy-start(bf16[2,512,1152]{2,1,0:T(8,128)(2,1)} %param.13) | copy-start | bytes 7077892
  475.1 333.8 %reduce-scatter.8.cloned.1.call-start = ((), (), s32[]{:S(2)}) async-start(), calls=%async_computation.10 | async-start | bytes 10948608 | tf_op jit(solution)/shard_map/reduce_scatter | solution.py:180
  577.9 116.6 %collective-permute-start.1 = (bf16[2,2304,512]{2,1,0:T(8,128)(2,1)}, bf16[2,2304,512]{2,1,0:T(8,128)(2,1)}, u32[]{:S(2)}, u32[]{:S(2)}) collective-permute-start(bf16[2,2304,512]{2,1,0:T(8,128)(2,1)} %pad_maximum_fusion.2), channel_id=1, source_target_pairs={{0,16},{16,0},{1,17},{17,1},{2,18},{18,2},{3,19},{19,3},{4,20},{20... | collective-permute-start | bytes 14155784 | tf_op jit(solution)/shard_map/ppermute | solution.py:186
  577.9 251.1 %all-gather.18.cloned.1.call-start = ((), (), s32[]{:S(2)}) async-start(), calls=%async_computation.7 | async-start | bytes 1824768 | tf_op jit(solution)/shard_map/all_gather | solution.py:321
  745.4 26.6 %copy-start.42 = (bf16[2,1152]{1,0:T(2,128)(2,1)S(1)}, bf16[2,1152]{1,0:T(2,128)(2,1)}, u32[]{:S(2)}) copy-start(bf16[2,1152]{1,0:T(2,128)(2,1)} %get-tuple-element.47) | copy-start | bytes 13828
  745.4 26.6 %copy-start.41 = (bf16[2,1152]{1,0:T(2,128)(2,1)S(1)}, bf16[2,1152]{1,0:T(2,128)(2,1)}, u32[]{:S(2)}) copy-start(bf16[2,1152]{1,0:T(2,128)(2,1)} %get-tuple-element.43) | copy-start | bytes 13828
  772.8 204.2 %reduce-scatter.4.cloned.1.call-start = ((), (), s32[]{:S(2)}) async-start(), calls=%async_computation.8 | async-start | bytes 10948608 | tf_op jit(solution)/shard_map/reduce_scatter | solution.py:172
  808.2 187.4 %all-gather.24.cloned.1.call-start = ((), (), s32[]{:S(2)}) async-start(), calls=%async_computation.13 | async-start | bytes 1658880 | tf_op jit(solution)/shard_map/all_gather | solution.py:173
  808.8 206.5 %all-gather.20.cloned.1.call-start = ((), (), s32[]{:S(2)}) async-start(), calls=%async_computation.11 | async-start | bytes 1658880 | tf_op jit(solution)/shard_map/all_gather | solution.py:181
  809.4 225.7 %all-gather.22.cloned.1.call-start = ((), (), s32[]{:S(2)}) async-start(), calls=%async_computation.12 | async-start | bytes 1658880 | tf_op jit(solution)/shard_map/all_gather | solution.py:173
  838.2 143.6 %copy-start.18 = (bf16[32,144]{1,0:T(8,128)(2,1)S(1)}, bf16[32,144]{1,0:T(8,128)(2,1)}, u32[]{:S(2)}) copy-start(bf16[32,144]{1,0:T(8,128)(2,1)} %copy-done.17) | copy-start | bytes 27652
  (33 other events, 289.5 us)
Sparse Core Ops, SparseCore 0:
  37.7 92.6 all-reduce.3
Sparse Core Ops, SparseCore 1:
  42.0 85.9 all-gather.11
  131.7 108.0 all-gather.13
  243.6 96.7 all-gather.15
  475.1 143.5 reduce-scatter.5
  625.9 144.0 reduce-scatter.7
  773.8 55.2 all-gather.17
  836.0 140.9 reduce-scatter.3
  978.5 17.1 all-gather.23
  997.1 18.1 all-gather.19
  1016.9 18.1 all-gather.21
